TPU v7x, 32 devices: a whole 2x2x4 slice. The times are simulated.
32 devices in a mesh: exp: 16 (over z, y, core), hid: 2 (over x).
Axes of the slice: x: 2, y: 2, z: 4, core: 2. Of those that a mesh axis runs over, the one named last changes fastest.
Arguments:
- tokens: bfloat16 [128, 2048], P(('exp', 'hid')), may hold values from -6 to 6
- grad_out: bfloat16 [128, 2048], P(('exp', 'hid')), may hold values from -3 to 3
- router_logits: float32 [128, 16], P(('exp', 'hid')), may hold values from -12 to 330
- selected: int32 [128, 8], P(('exp', 'hid')), may hold values from 0 to 15, as said below
- router_w: bfloat16 [2048, 16], replicated, may hold values from -0.59765625 to 0.59765625
- w_gate: bfloat16 [32, 2048, 384], P(('exp', 'hid')), may hold values from -0.125 to 0.125
- w_up: bfloat16 [32, 2048, 384], P(('exp', 'hid')), may hold values from -0.125 to 0.125
- w_down: bfloat16 [32, 384, 2048], P(('exp', 'hid')), may hold values from -0.21875 to 0.21875
Outputs:
- x_grad: bfloat16 [128, 2048], P(('exp', 'hid'))
- router_grad: float32 [2048, 16], P(('exp', 'hid'))
Inputs may be any that keep to these rules, and one draw needn't show every extreme that they name: `selected`: each row names 8 different experts; within each aligned block of 8 rows (the tokens of one index of exp) no expert is named by more than 8 rows, and in every block some expert is named by exactly 8 rows.
All inputs are finite; a program needn't handle non-finite values.
Results may differ from a plain program's by a relative error of at most 0.0075.
Values may be sent and summed in bfloat16 or wider, within the bound.
No kernel may reach another device: no remote copies, remote signals or barrier semaphores. Data moves between devices by JAX's collectives and lax.ppermute only.
A program may use at most 64 MiB of HBM per device.

v0:
```python
import functools

import jax
import jax.numpy as jnp
from jax import lax
from jax.experimental import pallas as pl
from jax.experimental.pallas import tpu as pltpu
from jax.sharding import PartitionSpec as P

AXES = ("exp", "hid")
LANES = 128
PIECES = 4
SCORE_PIECES = 2
VMEM_SPEC = pl.BlockSpec(memory_space=pltpu.VMEM)
HBM_SPEC = pl.BlockSpec(memory_space=pltpu.HBM)
F32 = jnp.float32
BF16 = jnp.bfloat16
NT = (((1,), (1,)), ((), ()))
TN = (((0,), (0,)), ((), ()))
PARAMS = pltpu.CompilerParams(vmem_limit_bytes=24 * 2**20)


def stage_masks(exp_size, hid_size):
    hid_bits = hid_size.bit_length() - 1
    all_bits = (exp_size * hid_size).bit_length() - 1
    core = hid_bits
    first = list(range(max(core + 1, all_bits - 2), all_bits))
    middle = [b for b in range(all_bits) if b != core and b not in first]
    groups = [first] + [middle[i : i + 2] for i in range(0, len(middle), 2)]
    return groups, core


def group_masks(bits):
    masks = [0]
    for bit in bits:
        masks = masks + [m | (1 << bit) for m in masks]
    return masks


def swap(block, mask, count):
    return lax.ppermute(block, AXES, [(i, i ^ mask) for i in range(count)])


def place_mask(place, bits):
    total = jnp.zeros_like(place)
    for digit, bit in enumerate(bits):
        total = total | (((place >> digit) & 1) << bit)
    return total


def own_index():
    return lax.axis_index("exp") * lax.axis_size("hid") + lax.axis_index("hid")


def in_hbm(*arrays):
    return tuple(pltpu.with_memory_space_constraint(a, pltpu.HBM) for a in arrays)


def softmax_f32(values):
    raised = jnp.exp(values - jnp.max(values, axis=-1, keepdims=True))
    return raised / jnp.sum(raised, axis=-1, keepdims=True)


def prep_kernel(tokens_in, grad_in, logits_in, chosen_in, out_ref, tokens_ref, grad_ref, logits_ref, chosen_ref,
                rows_ref, sems):
    copies = [
        pltpu.make_async_copy(src, dst, sems.at[i])
        for i, (src, dst) in enumerate(
            [(logits_in, logits_ref), (chosen_in, chosen_ref), (tokens_in, tokens_ref), (grad_in, grad_ref)]
        )
    ]
    for copy in copies:
        copy.start()
    copies[0].wait()
    copies[1].wait()
    tok, width = tokens_ref.shape
    logits = logits_ref[...]
    chosen = chosen_ref[...]
    experts = logits.shape[1]
    ids = lax.broadcasted_iota(jnp.int32, logits.shape, 1)
    hit = ids == chosen[:, 0:1]
    for k in range(1, chosen.shape[1]):
        hit = hit | (ids == chosen[:, k : k + 1])
    top = jnp.max(jnp.where(hit, logits, -jnp.inf), axis=1, keepdims=True)
    raised = jnp.where(hit, jnp.exp(jnp.minimum(logits - top, 0.0)), 0.0)
    parts = [raised / jnp.sum(raised, axis=1, keepdims=True)]
    rest = softmax_f32(logits)
    for _ in range(PIECES - 1):
        parts.append(rest)
        rest = rest - rest.astype(BF16).astype(F32)
    lanes = out_ref.shape[1] - width
    extras = jnp.zeros((tok, lanes), F32)
    row = lax.broadcasted_iota(jnp.int32, (experts, lanes), 0)
    lane = lax.broadcasted_iota(jnp.int32, (experts, lanes), 1)
    for k, part in enumerate(parts):
        place = jnp.where(lane == row + k * experts, 1.0, 0.0).astype(BF16)
        extras = extras + jnp.dot(part.astype(BF16), place, preferred_element_type=F32)
    copies[2].wait()
    copies[3].wait()
    rows_ref[0:tok, :width] = tokens_ref[...].astype(F32)
    rows_ref[tok:, :width] = grad_ref[...].astype(F32)
    rows_ref[0:tok, width:] = extras
    rows_ref[tok:, width:] = jnp.zeros((tok, lanes), F32)
    out_ref[...] = rows_ref[...].astype(BF16)


def load_kernel(chunks, after_ref, *refs):
    count = (len(refs) - 1) // 2
    sems = refs[-1]
    copies = []
    for src, dst in zip(refs[:count], refs[count : 2 * count]):
        size = src.shape[1] // chunks
        for c in range(chunks):
            part = (slice(None), pl.ds(c * size, size))
            copies.append(pltpu.make_async_copy(src.at[part], dst.at[part], sems.at[len(copies)]))
    for copy in copies:
        copy.start()
    for copy in copies:
        copy.wait()


def put_scores(out_ref, scores_ref, width):
    rows = out_ref.shape[0]
    for c in range((out_ref.shape[1] - width) // LANES):
        out_ref[:, width + c * LANES : width + (c + 1) * LANES] = scores_ref[c * rows : (c + 1) * rows, :].astype(BF16)


def get_scores(in_ref, scores_ref, base, size, width):
    rows = in_ref.shape[0]
    for c in range(-(-size // rows)):
        here = min(rows, size - c * rows)
        tall = min(rows, -(-here // 16) * 16)
        block = in_ref[0:tall, width + c * LANES : width + (c + 1) * LANES].astype(F32)
        scores_ref[base + c * rows : base + c * rows + here, :] = block[:here]


def half_kernel(bits, swap_mask, last, buf_ref, gate_ref, up_ref, down_ref, *rest):
    width = gate_ref.shape[1]
    experts_width = buf_ref.shape[1] - width
    own = own_index()
    expert = own // 2
    rows = buf_ref.shape[0]
    if last:
        base_ref, out_ref, pieces_ref, score_ref, padded_ref = rest
        score_ref[...] = base_ref[...]
    else:
        out_ref, score_ref = rest
        score_ref[...] = jnp.zeros(score_ref.shape, F32)
    tokens = score_ref.shape[1]
    step = min(rows, 128)

    def one(index):
        start = pl.multiple_of(index * step, step)
        block = buf_ref[pl.ds(start, step), :]
        act = block[:, :width]
        extras = block[:, width:].astype(F32)
        lane = lax.broadcasted_iota(jnp.int32, (step, experts_width), 1)
        column = jnp.sum(jnp.where(lane == expert, extras, 0.0), axis=1, keepdims=True)
        gate_pre = jnp.dot(act, gate_ref[0], preferred_element_type=F32)
        up_pre = jnp.dot(act, up_ref[0], preferred_element_type=F32)
        back = lax.dot_general(act, down_ref[0], NT, preferred_element_type=F32)
        back = pltpu.roll(back, step - 4, 0)
        sig = jax.nn.sigmoid(gate_pre)
        act_gate = gate_pre * sig
        score = jnp.sum(act_gate * up_pre * back, axis=1, keepdims=True)
        weighted = column * back
        grad_gate = weighted * up_pre * sig * (1.0 + gate_pre * (1.0 - sig))
        grad_up = weighted * act_gate

        def compact(value):
            pairs = value.reshape(step // 16, 16, value.shape[1])
            low = pairs[:, :8]
            high = pairs[:, 8:]
            high = jnp.concatenate([high[:, 4:], high[:, :4]], axis=1)
            sub = lax.broadcasted_iota(jnp.int32, low.shape, 1)
            return jnp.where(sub < 4, low, high).reshape(step // 2, value.shape[1]).astype(BF16)

        total = lax.dot_general(compact(grad_gate), gate_ref[0], NT, preferred_element_type=F32)
        total = total + lax.dot_general(compact(grad_up), up_ref[0], NT, preferred_element_type=F32)
        out_start = pl.multiple_of(index * (step // 2), step // 2)
        out_ref[pl.ds(out_start, step // 2), 0:width] = total.astype(out_ref.dtype)

        row = lax.broadcasted_iota(jnp.int32, (step, tokens), 0) + start
        token = lax.broadcasted_iota(jnp.int32, (step, tokens), 1)
        whole = (place_mask(row >> 3, bits) ^ (own ^ swap_mask)) * 4 + (row & 7)
        here = (whole == token) & ((row & 7) < 4)
        score_ref[...] += jnp.sum(jnp.where(here, score, 0.0), axis=0, keepdims=True)

    if rows == step:
        one(0)
    else:
        pl.loop(0, rows // step)(one)
    if last:
        blocks = tokens // LANES
        padded_ref[...] = jnp.zeros(padded_ref.shape, F32)
        value = score_ref[...]
        for piece in range(SCORE_PIECES):
            rounded = value.astype(BF16).astype(F32)
            for b in range(blocks):
                padded_ref[piece * blocks + b : piece * blocks + b + 1, :] = rounded[:, b * LANES : (b + 1) * LANES]
            value = value - rounded
        pieces_ref[...] = padded_ref[0 : pieces_ref.shape[0], :]
        put_scores(out_ref, padded_ref, width)


def add_kernel(arrivals, radix, *refs):
    kept_ref, pieces_ref = refs[0], refs[1]
    arrived = refs[2 : 2 + arrivals]
    outs = refs[2 + arrivals :]
    next_kept_ref, next_pieces_ref = outs[0], outs[1]
    sends = outs[2 : 1 + radix]
    total_ref, scores_ref = outs[1 + radix :]
    width = kept_ref.shape[1]
    size = pieces_ref.shape[0]
    total = kept_ref[...]
    for ref in arrived:
        total = total + ref[:, 0:width].astype(F32)
    total_ref[...] = total
    if scores_ref.shape[0] > next_pieces_ref.shape[0]:
        scores_ref[...] = jnp.zeros(scores_ref.shape, F32)
    scores_ref[0:size, :] = pieces_ref[...]
    for j, ref in enumerate(arrived):
        get_scores(ref, scores_ref, (j + 1) * size, size, width)
    rows = next_kept_ref.shape[0]
    next_kept_ref[...] = total_ref[0:rows, :]
    next_pieces_ref[...] = scores_ref[0 : next_pieces_ref.shape[0], :]
    for j, ref in enumerate(sends):
        ref[:, 0:width] = total_ref[(j + 1) * rows : (j + 2) * rows, :].astype(BF16)
        put_scores(ref, scores_ref, width)


def final_kernel(arrivals, bits, back_bits, core_mask, *refs):
    buf_own_ref, buf_other_ref, router_ref, kept_ref, pieces_ref = refs[:5]
    arrived = refs[5 : 5 + arrivals]
    x_ref, grad_ref, scores_ref, lg_ref = refs[5 + arrivals :]
    experts, width = router_ref.shape
    half, buf_width = buf_own_ref.shape
    lanes = buf_width - width
    size = pieces_ref.shape[0]
    tok = kept_ref.shape[0]
    own = own_index()
    scores_ref[0:size, :] = pieces_ref[...]
    for j, ref in enumerate(arrived):
        get_scores(ref, scores_ref, (j + 1) * size, size, width)
    tokens = half * 2 // 8 * 4
    blocks = tokens // LANES
    wide = scores_ref.shape[0] // blocks
    sender = lax.broadcasted_iota(jnp.int32, (wide, experts), 0) // SCORE_PIECES
    ids = lax.broadcasted_iota(jnp.int32, (wide, experts), 1)
    pick = jnp.where(((place_mask(sender, back_bits) ^ own) >> 1) == ids, 1.0, 0.0).astype(BF16)
    lane = lax.broadcasted_iota(jnp.int32, (lanes, experts), 0)
    ids = lax.broadcasted_iota(jnp.int32, (lanes, experts), 1)
    tally = jnp.zeros((lanes, experts), F32)
    for k in range(1, PIECES):
        tally = tally + jnp.where(lane == ids + k * experts, 1.0, 0.0)
    rows_out = grad_ref.shape[1]
    first = own * rows_out
    column = pl.multiple_of(first // LANES * LANES, LANES)
    grad = jnp.zeros((experts, LANES), F32)
    for index, ref in enumerate((buf_own_ref, buf_other_ref)):
        picked = jnp.zeros((half, wide), F32)
        for b in range(blocks):
            row = lax.broadcasted_iota(jnp.int32, (half, LANES), 0)
            token = lax.broadcasted_iota(jnp.int32, (half, LANES), 1) + b * LANES
            whole = (place_mask(row >> 3, bits) ^ (own ^ (core_mask if index else 0))) * 4 + (row & 7)
            here = jnp.where((whole == token) & ((row & 7) < 4), 1.0, 0.0).astype(BF16)
            block = scores_ref[...] if blocks == 1 else scores_ref[pl.ds(b, wide, stride=blocks), :]
            picked = picked + lax.dot_general(here, block.astype(BF16), NT, preferred_element_type=F32)
        scores = jnp.dot(picked.astype(BF16), pick, preferred_element_type=F32)
        probs = jnp.dot(ref[:, width:], tally.astype(BF16), preferred_element_type=F32)
        mean = jnp.sum(probs * scores, axis=1, keepdims=True)
        logit_grad = probs * (scores - mean)
        if index == 0:
            lg_ref[...] = logit_grad[0:8]
        grad = grad + lax.dot_general(
            logit_grad.astype(BF16), ref[:, pl.ds(column, LANES)], TN, preferred_element_type=F32
        )
    shift = (LANES - (first - column)) % LANES
    grad_ref[...] = pltpu.roll(grad, shift, 1)[:, :rows_out]
    part = jnp.dot(lg_ref[...].astype(BF16), router_ref[...], preferred_element_type=F32)
    total = kept_ref[...]
    for ref in arrived:
        total = total + ref[:, 0:width].astype(F32)
    x_ref[...] = (total + part[:tok]).astype(BF16)


def on_device(tokens, grad_out, router_logits, selected, router_w, w_gate, w_up, w_down):
    tok, width = tokens.shape
    experts = router_logits.shape[1]
    hidden = w_gate.shape[2]
    exp_size = lax.axis_size("exp")
    hid_size = lax.axis_size("hid")
    count = exp_size * hid_size
    half = count // 2
    groups, core = stage_masks(exp_size, hid_size)
    core_mask = 1 << core
    bits = [b for group in groups for b in group]
    back_groups = [[core]] + groups[::-1]
    back_bits = [b for group in back_groups for b in group]
    token_count = count * tok
    lanes = -(-PIECES * experts // LANES) * LANES

    block = pl.pallas_call(
        prep_kernel,
        out_shape=jax.ShapeDtypeStruct((2 * tok, width + lanes), BF16),
        in_specs=[HBM_SPEC] * 4,
        out_specs=VMEM_SPEC,
        scratch_shapes=[
            pltpu.VMEM(tokens.shape, tokens.dtype),
            pltpu.VMEM(grad_out.shape, grad_out.dtype),
            pltpu.VMEM(router_logits.shape, router_logits.dtype),
            pltpu.VMEM(selected.shape, selected.dtype),
            pltpu.VMEM((2 * tok, width + lanes), F32),
            pltpu.SemaphoreType.DMA((4,)),
        ],
        compiler_params=PARAMS,
        name="prep",
    )(*in_hbm(tokens, grad_out, router_logits, selected))

    weights = in_hbm(w_gate, w_up, w_down)
    for index, group in enumerate(groups):
        if index == len(groups) - 1:
            chunks = 4
            weights = pl.pallas_call(
                functools.partial(load_kernel, chunks),
                out_shape=tuple(pltpu.VMEM(w.shape, w.dtype) for w in weights),
                in_specs=[pl.BlockSpec(memory_space=pl.ANY)] + [HBM_SPEC] * 3,
                out_specs=(VMEM_SPEC,) * 3,
                scratch_shapes=[pltpu.SemaphoreType.DMA((3 * chunks,))],
                compiler_params=pltpu.CompilerParams(vmem_limit_bytes=4 * 2**20),
                cost_estimate=pl.CostEstimate(flops=0, bytes_accessed=6 * width * hidden * 2, transcendentals=0),
                name="load",
            )(block, *weights)
        block = jnp.concatenate([block] + [swap(block, m, count) for m in group_masks(group)[1:]], axis=0)
    other = swap(block, core_mask, count)

    cost = pl.CostEstimate(
        flops=2 * half * 8 * width * hidden * 4,
        bytes_accessed=3 * width * hidden * 2 + half * 8 * width * 2,
        transcendentals=half * 8 * hidden,
    )
    unit_rows = SCORE_PIECES * token_count // LANES
    kept, score = pl.pallas_call(
        functools.partial(half_kernel, bits, 0, False),
        out_shape=(
            jax.ShapeDtypeStruct((half * tok, width), F32),
            jax.ShapeDtypeStruct((1, token_count), F32),
        ),
        in_specs=[VMEM_SPEC] * 4,
        out_specs=(VMEM_SPEC, VMEM_SPEC),
        compiler_params=PARAMS,
        cost_estimate=cost,
        name="half_own",
    )(block, *weights)
    extra = -(-unit_rows // (half * tok)) * LANES
    message, pieces = pl.pallas_call(
        functools.partial(half_kernel, bits, core_mask, True),
        out_shape=(
            jax.ShapeDtypeStruct((half * tok, width + extra), BF16),
            jax.ShapeDtypeStruct((unit_rows, LANES), F32),
        ),
        in_specs=[VMEM_SPEC] * 5,
        out_specs=(VMEM_SPEC, VMEM_SPEC),
        scratch_shapes=[
            pltpu.VMEM((1, token_count), F32),
            pltpu.VMEM((max(half * tok * extra // LANES, unit_rows), LANES), F32),
        ],
        compiler_params=PARAMS,
        cost_estimate=cost,
        name="half_other",
    )(other, *weights, score)

    arrived = [swap(message, core_mask, count)]
    for group in groups[::-1]:
        masks = group_masks(group)
        radix = len(masks)
        rows = kept.shape[0]
        next_rows = rows // radix
        size = pieces.shape[0] * (1 + len(arrived))
        extra = -(-size // next_rows) * LANES
        sends = [jax.ShapeDtypeStruct((next_rows, width + extra), BF16)] * (radix - 1)
        outs = pl.pallas_call(
            functools.partial(add_kernel, len(arrived), radix),
            out_shape=[
                jax.ShapeDtypeStruct((next_rows, width), F32),
                jax.ShapeDtypeStruct((size, LANES), F32),
            ]
            + sends,
            in_specs=[VMEM_SPEC] * (2 + len(arrived)),
            out_specs=[VMEM_SPEC] * (1 + radix),
            scratch_shapes=[
                pltpu.VMEM((rows, width), F32),
                pltpu.VMEM((max(next_rows * extra // LANES, size), LANES), F32),
            ],
            compiler_params=PARAMS,
            name="add",
        )(kept, pieces, *arrived)
        kept, pieces = outs[0], outs[1]
        arrived = [swap(piece, m, count) for piece, m in zip(outs[2:], masks[1:])]

    x_grad, grad = pl.pallas_call(
        functools.partial(final_kernel, len(arrived), bits, back_bits, core_mask),
        out_shape=(
            jax.ShapeDtypeStruct((tok, width), BF16),
            jax.ShapeDtypeStruct((experts, width // count), F32),
        ),
        in_specs=[VMEM_SPEC] * (5 + len(arrived)),
        out_specs=(VMEM_SPEC, VMEM_SPEC),
        scratch_shapes=[
            pltpu.VMEM((pieces.shape[0] * (1 + len(arrived)), LANES), F32),
            pltpu.VMEM((8, experts), F32),
        ],
        compiler_params=PARAMS,
        name="final",
    )(block, other, router_w.T, kept, pieces, *arrived)
    return (x_grad, grad.T)


def solution(mesh):
    rows = P(AXES, None)
    units = P(AXES, None, None)
    return jax.shard_map(
        on_device,
        mesh=mesh,
        in_specs=(rows, rows, rows, rows, P(), units, units, units),
        out_specs=(rows, rows),
        check_vma=False,
    )
```

profile of v0, /device:TPU:0, one launch (start us, length us, event | category | flops | bytes accessed | tf_op | source)
XLA Modules:
  0.0 45.9 jit_solution(4281299135992122837)
XLA Ops:
  0.6 1.1 %prep.1 = bf16[8,2176]{1,0:T(8,128)(2,1)S(1)} custom-call(bf16[4,2048]{1,0:T(4,128)(2,1)} %tokens_in.1, bf16[4,2048]{1,0:T(4,128)(2,1)} %grad_in.1, f32[4,16]{1,0:T(4,128)} %logits_in.1, s32[4,8]{1,0:T(4,128)} %chosen_in.1), custom_call_target="tpu_custom_call" | custom-call | tf_op jit(solution)/shard_map/prep/pallas_call | solution.py:303
  1.8 3.1 %collective-permute-start = (bf16[8,2176]{1,0:T(8,128)(2,1)S(1)}, bf16[8,2176]{1,0:T(8,128)(2,1)S(1)}, u32[]{:S(2)}, u32[]{:S(2)}) collective-permute-start(bf16[8,2176]{1,0:T(8,128)(2,1)S(1)} %prep.1), channel_id=1, source_target_pairs={{0,8},{1,9},{2,10},{3,11},{4,12},{5,13},{6,14},{7,15},{8,0},{9,1},... | collective-permute-start | bytes 104456 | tf_op jit(solution)/shard_map/ppermute | solution.py:41
  4.8 2.6 %collective-permute-start.1 = (bf16[8,2176]{1,0:T(8,128)(2,1)S(1)}, bf16[8,2176]{1,0:T(8,128)(2,1)S(1)}, u32[]{:S(2)}, u32[]{:S(2)}) collective-permute-start(bf16[8,2176]{1,0:T(8,128)(2,1)S(1)} %prep.1), channel_id=1, source_target_pairs={{0,16},{1,17},{2,18},{3,19},{4,20},{5,21},{6,22},{7,23},{8,24},{9,... | collective-permute-start | bytes 104456 | tf_op jit(solution)/shard_map/ppermute | solution.py:41
  7.4 2.9 %collective-permute-done.1 = bf16[8,2176]{1,0:T(8,128)(2,1)S(1)} collective-permute-done((bf16[8,2176]{1,0:T(8,128)(2,1)S(1)}, bf16[8,2176]{1,0:T(8,128)(2,1)S(1)}, u32[]{:S(2)}, u32[]{:S(2)}) %collective-permute-start.1) | collective-permute-done | bytes 34848 | tf_op jit(solution)/shard_map/ppermute | solution.py:41
  10.3 2.9 %collective-permute-done.2 = bf16[8,2176]{1,0:T(8,128)(2,1)S(1)} collective-permute-done((bf16[8,2176]{1,0:T(8,128)(2,1)S(1)}, bf16[8,2176]{1,0:T(8,128)(2,1)S(1)}, u32[]{:S(2)}, u32[]{:S(2)}) %collective-permute-start.2) | collective-permute-done | bytes 34848 | tf_op jit(solution)/shard_map/ppermute | solution.py:41
  13.2 1.6 %collective-permute-start.3 = (bf16[32,2176]{1,0:T(8,128)(2,1)S(1)}, bf16[32,2176]{1,0:T(8,128)(2,1)S(1)}, u32[]{:S(2)}, u32[]{:S(2)}) collective-permute-start(bf16[32,2176]{1,0:T(8,128)(2,1)S(1)} %pad_maximum_fusion.after_ref), channel_id=1, source_target_pairs={{0,1},{1,0},{2,3},{3,2},{4,5},{5,4},{6,7},{7,6},{8,9},{9,8},{10,11... | collective-permute-start | bytes 417800 | tf_op jit(solution)/shard_map/ppermute | solution.py:41
  14.7 1.5 %collective-permute-start.4 = (bf16[32,2176]{1,0:T(8,128)(2,1)S(1)}, bf16[32,2176]{1,0:T(8,128)(2,1)S(1)}, u32[]{:S(2)}, u32[]{:S(2)}) collective-permute-start(bf16[32,2176]{1,0:T(8,128)(2,1)S(1)} %pad_maximum_fusion.after_ref), channel_id=1, source_target_pairs={{0,4},{1,5},{2,6},{3,7},{4,0},{5,1},{6,2},{7,3},{8,12},{9,13},{10,... | collective-permute-start | bytes 417800 | tf_op jit(solution)/shard_map/ppermute | solution.py:41
  16.3 0.5 %collective-permute-start.5 = (bf16[32,2176]{1,0:T(8,128)(2,1)S(1)}, bf16[32,2176]{1,0:T(8,128)(2,1)S(1)}, u32[]{:S(2)}, u32[]{:S(2)}) collective-permute-start(bf16[32,2176]{1,0:T(8,128)(2,1)S(1)} %pad_maximum_fusion.after_ref), channel_id=1, source_target_pairs={{0,5},{1,4},{2,7},{3,6},{4,1},{5,0},{6,3},{7,2},{8,13},{9,12},{10,... | collective-permute-start | bytes 417800 | tf_op jit(solution)/shard_map/ppermute | solution.py:41
  16.8 2.7 %collective-permute-done.3 = bf16[32,2176]{1,0:T(8,128)(2,1)S(1)} collective-permute-done((bf16[32,2176]{1,0:T(8,128)(2,1)S(1)}, bf16[32,2176]{1,0:T(8,128)(2,1)S(1)}, u32[]{:S(2)}, u32[]{:S(2)}) %collective-permute-start.3) | collective-permute-done | bytes 139296 | tf_op jit(solution)/shard_map/ppermute | solution.py:41
  19.5 1.3 %collective-permute-done.4 = bf16[32,2176]{1,0:T(8,128)(2,1)S(1)} collective-permute-done((bf16[32,2176]{1,0:T(8,128)(2,1)S(1)}, bf16[32,2176]{1,0:T(8,128)(2,1)S(1)}, u32[]{:S(2)}, u32[]{:S(2)}) %collective-permute-start.4) | collective-permute-done | bytes 139296 | tf_op jit(solution)/shard_map/ppermute | solution.py:41
  20.8 1.5 %collective-permute-done.5 = bf16[32,2176]{1,0:T(8,128)(2,1)S(1)} collective-permute-done((bf16[32,2176]{1,0:T(8,128)(2,1)S(1)}, bf16[32,2176]{1,0:T(8,128)(2,1)S(1)}, u32[]{:S(2)}, u32[]{:S(2)}) %collective-permute-start.5) | collective-permute-done | bytes 139296 | tf_op jit(solution)/shard_map/ppermute | solution.py:41
  22.2 0.1 collective-permute-start.6
  22.3 2.4 %load.1 = (bf16[1,2048,384]{2,1,0:T(8,128)(2,1)S(1)}, bf16[1,2048,384]{2,1,0:T(8,128)(2,1)S(1)}, bf16[1,384,2048]{2,1,0:T(8,128)(2,1)S(1)}) custom-call(bf16[32,2176]{1,0:T(8,128)(2,1)S(1)} %pad_maximum_fusion.after_ref, bf16[1,2048,384]{2,1,0:T(8,128)(2,1)} %refs_0_.1, bf16[1,2048,384]{2,1,0:T(8,128)(2,1)} %refs_1_.1, bf16[1,384,2048]{2,1,0:T(8,128)(2,1)} %refs_2_.1), custom_call_target="tpu_custom_call" | custom-call | bytes 9437184 | tf_op jit(solution)/shard_map/load/pallas_call | solution.py:324
  24.7 2.3 %half_own.1 = (f32[64,2048]{1,0:T(8,128)S(1)}, f32[1,128]{1,0:T(1,128)S(1)}) custom-call(bf16[128,2176]{1,0:T(8,128)(2,1)S(1)} %constant_dynamic-update-slice_fusion.buf_ref.refs_0_, bf16[1,2048,384]{2,1,0:T(8,128)(2,1)S(1)} %get-tuple-element.21.gate_ref, bf16[1,2048,384]{2,1,0:T(8,128)(2,1)S(1)} %get-tuple-element.22.up_ref, ...), custom_call_target="tpu_custom_call" | custom-call | flops 805306368 | bytes 5242880 | tf_op jit(solution)/shard_map/half_own/pallas_call | solution.py:343
  27.1 0.0 copy-start
  27.1 2.4 %half_other.1 = (bf16[64,2176]{1,0:T(8,128)(2,1)S(1)}, f32[2,128]{1,0:T(2,128)S(1)}) custom-call(bf16[128,2176]{1,0:T(8,128)(2,1)S(1)} %collective-permute-done.6.buf_ref.refs_1_, bf16[1,2048,384]{2,1,0:T(8,128)(2,1)S(1)} %get-tuple-element.21.gate_ref, bf16[1,2048,384]{2,1,0:T(8,128)(2,1)S(1)} %get-tuple-element.22.up_ref, ...), custom_call_target="tpu_custom_call" | custom-call | flops 805306368 | bytes 5242880 | tf_op jit(solution)/shard_map/half_other/pallas_call | solution.py:356
  29.5 0.6 %collective-permute-start.7 = (bf16[64,2176]{1,0:T(8,128)(2,1)S(1)}, bf16[64,2176]{1,0:T(8,128)(2,1)S(1)}, u32[]{:S(2)}, u32[]{:S(2)}) collective-permute-start(bf16[64,2176]{1,0:T(8,128)(2,1)S(1)} %get-tuple-element.27), channel_id=1, source_target_pairs={{0,2},{1,3},{2,0},{3,1},{4,6},{5,7},{6,4},{7,5},{8,10},{9,11},{10,... | collective-permute-start | bytes 835592 | tf_op jit(solution)/shard_map/ppermute | solution.py:41
  30.0 1.2 %collective-permute-done.7.refs_2_ = bf16[64,2176]{1,0:T(8,128)(2,1)S(1)} collective-permute-done((bf16[64,2176]{1,0:T(8,128)(2,1)S(1)}, bf16[64,2176]{1,0:T(8,128)(2,1)S(1)}, u32[]{:S(2)}, u32[]{:S(2)}) %collective-permute-start.7) | collective-permute-done | bytes 278560 | tf_op jit(solution)/shard_map/ppermute | solution.py:41
  31.2 0.1 add.2
  31.3 0.6 %collective-permute-start.8 = (bf16[16,2176]{1,0:T(8,128)(2,1)S(1)}, bf16[16,2176]{1,0:T(8,128)(2,1)S(1)}, u32[]{:S(2)}, u32[]{:S(2)}) collective-permute-start(bf16[16,2176]{1,0:T(8,128)(2,1)S(1)} %get-tuple-element.30), channel_id=1, source_target_pairs={{0,1},{1,0},{2,3},{3,2},{4,5},{5,4},{6,7},{7,6},{8,9},{9,8},{10,11... | collective-permute-start | bytes 208904 | tf_op jit(solution)/shard_map/ppermute | solution.py:41
  31.9 0.6 %collective-permute-start.9 = (bf16[16,2176]{1,0:T(8,128)(2,1)S(1)}, bf16[16,2176]{1,0:T(8,128)(2,1)S(1)}, u32[]{:S(2)}, u32[]{:S(2)}) collective-permute-start(bf16[16,2176]{1,0:T(8,128)(2,1)S(1)} %get-tuple-element.31), channel_id=1, source_target_pairs={{0,4},{1,5},{2,6},{3,7},{4,0},{5,1},{6,2},{7,3},{8,12},{9,13},{10,... | collective-permute-start | bytes 208904 | tf_op jit(solution)/shard_map/ppermute | solution.py:41
  32.5 2.4 %collective-permute-start.10 = (bf16[16,2176]{1,0:T(8,128)(2,1)S(1)}, bf16[16,2176]{1,0:T(8,128)(2,1)S(1)}, u32[]{:S(2)}, u32[]{:S(2)}) collective-permute-start(bf16[16,2176]{1,0:T(8,128)(2,1)S(1)} %get-tuple-element.32), channel_id=1, source_target_pairs={{0,5},{1,4},{2,7},{3,6},{4,1},{5,0},{6,3},{7,2},{8,13},{9,12},{10,... | collective-permute-start | bytes 208904 | tf_op jit(solution)/shard_map/ppermute | solution.py:41
  34.9 1.0 %collective-permute-done.8.refs_2_ = bf16[16,2176]{1,0:T(8,128)(2,1)S(1)} collective-permute-done((bf16[16,2176]{1,0:T(8,128)(2,1)S(1)}, bf16[16,2176]{1,0:T(8,128)(2,1)S(1)}, u32[]{:S(2)}, u32[]{:S(2)}) %collective-permute-start.8) | collective-permute-done | bytes 69664 | tf_op jit(solution)/shard_map/ppermute | solution.py:41
  35.9 0.6 %collective-permute-done.9.refs_3_ = bf16[16,2176]{1,0:T(8,128)(2,1)S(1)} collective-permute-done((bf16[16,2176]{1,0:T(8,128)(2,1)S(1)}, bf16[16,2176]{1,0:T(8,128)(2,1)S(1)}, u32[]{:S(2)}, u32[]{:S(2)}) %collective-permute-start.9) | collective-permute-done | bytes 69664 | tf_op jit(solution)/shard_map/ppermute | solution.py:41
  36.5 1.3 %collective-permute-done.10.refs_4_ = bf16[16,2176]{1,0:T(8,128)(2,1)S(1)} collective-permute-done((bf16[16,2176]{1,0:T(8,128)(2,1)S(1)}, bf16[16,2176]{1,0:T(8,128)(2,1)S(1)}, u32[]{:S(2)}, u32[]{:S(2)}) %collective-permute-start.10) | collective-permute-done | bytes 69664 | tf_op jit(solution)/shard_map/ppermute | solution.py:41
  37.7 0.1 add.3
  37.8 0.1 collective-permute-start.11
  37.9 1.1 %collective-permute-start.12 = (bf16[4,2560]{1,0:T(4,128)(2,1)S(1)}, bf16[4,2560]{1,0:T(4,128)(2,1)S(1)}, u32[]{:S(2)}, u32[]{:S(2)}) collective-permute-start(bf16[4,2560]{1,0:T(4,128)(2,1)S(1)} %get-tuple-element.36), channel_id=1, source_target_pairs={{0,16},{1,17},{2,18},{3,19},{4,20},{5,21},{6,22},{7,23},{8,24},{9,... | collective-permute-start | bytes 61448 | tf_op jit(solution)/shard_map/ppermute | solution.py:41
  39.0 3.2 %collective-permute-start.13 = (bf16[4,2560]{1,0:T(4,128)(2,1)S(1)}, bf16[4,2560]{1,0:T(4,128)(2,1)S(1)}, u32[]{:S(2)}, u32[]{:S(2)}) collective-permute-start(bf16[4,2560]{1,0:T(4,128)(2,1)S(1)} %get-tuple-element.37), channel_id=1, source_target_pairs={{0,24},{1,25},{2,26},{3,27},{4,28},{5,29},{6,30},{7,31},{8,16},{9,... | collective-permute-start | bytes 61448 | tf_op jit(solution)/shard_map/ppermute | solution.py:41
  42.3 0.4 collective-permute-done.12.refs_6_
  42.7 1.9 %collective-permute-done.13.refs_7_ = bf16[4,2560]{1,0:T(4,128)(2,1)S(1)} collective-permute-done((bf16[4,2560]{1,0:T(4,128)(2,1)S(1)}, bf16[4,2560]{1,0:T(4,128)(2,1)S(1)}, u32[]{:S(2)}, u32[]{:S(2)}) %collective-permute-start.13) | collective-permute-done | bytes 20512 | tf_op jit(solution)/shard_map/ppermute | solution.py:41
  44.6 1.2 %final.1 = (bf16[4,2048]{1,0:T(4,128)(2,1)}, f32[16,64]{1,0:T(8,128)}) custom-call(bf16[128,2176]{1,0:T(8,128)(2,1)S(1)} %constant_dynamic-update-slice_fusion.buf_ref.refs_0_, bf16[128,2176]{1,0:T(8,128)(2,1)S(1)} %collective-permute-done.6.buf_ref.refs_1_, bf16[16,2048]{1,0:T(8,128)(2,1)S(1)} %bitcast.2, f32[4,2048]{1,0:T(4,128)S(1)} %get-tuple-element.33.refs_3_, ...), custom_call_target="tpu_custom_call" | custom-call | tf_op jit(solution)/shard_map/final/pallas_call | solution.py:401
  (13 shorter events, 0.1 us)
Async XLA Ops:
  1.8 5.7 %collective-permute-start = (bf16[8,2176]{1,0:T(8,128)(2,1)S(1)}, bf16[8,2176]{1,0:T(8,128)(2,1)S(1)}, u32[]{:S(2)}, u32[]{:S(2)}) collective-permute-start(bf16[8,2176]{1,0:T(8,128)(2,1)S(1)} %prep.1), channel_id=1, source_target_pairs={{0,8},{1,9},{2,10},{3,11},{4,12},{5,13},{6,14},{7,15},{8,0},{9,1},... | collective-permute-start | bytes 104456 | tf_op jit(solution)/shard_map/ppermute | solution.py:41
  4.8 5.5 %collective-permute-start.1 = (bf16[8,2176]{1,0:T(8,128)(2,1)S(1)}, bf16[8,2176]{1,0:T(8,128)(2,1)S(1)}, u32[]{:S(2)}, u32[]{:S(2)}) collective-permute-start(bf16[8,2176]{1,0:T(8,128)(2,1)S(1)} %prep.1), channel_id=1, source_target_pairs={{0,16},{1,17},{2,18},{3,19},{4,20},{5,21},{6,22},{7,23},{8,24},{9,... | collective-permute-start | bytes 104456 | tf_op jit(solution)/shard_map/ppermute | solution.py:41
  7.4 5.7 %collective-permute-start.2 = (bf16[8,2176]{1,0:T(8,128)(2,1)S(1)}, bf16[8,2176]{1,0:T(8,128)(2,1)S(1)}, u32[]{:S(2)}, u32[]{:S(2)}) collective-permute-start(bf16[8,2176]{1,0:T(8,128)(2,1)S(1)} %prep.1), channel_id=1, source_target_pairs={{0,24},{1,25},{2,26},{3,27},{4,28},{5,29},{6,30},{7,31},{8,16},{9,... | collective-permute-start | bytes 104456 | tf_op jit(solution)/shard_map/ppermute | solution.py:41
  13.2 6.3 %collective-permute-start.3 = (bf16[32,2176]{1,0:T(8,128)(2,1)S(1)}, bf16[32,2176]{1,0:T(8,128)(2,1)S(1)}, u32[]{:S(2)}, u32[]{:S(2)}) collective-permute-start(bf16[32,2176]{1,0:T(8,128)(2,1)S(1)} %pad_maximum_fusion.after_ref), channel_id=1, source_target_pairs={{0,1},{1,0},{2,3},{3,2},{4,5},{5,4},{6,7},{7,6},{8,9},{9,8},{10,11... | collective-permute-start | bytes 417800 | tf_op jit(solution)/shard_map/ppermute | solution.py:41
  14.7 6.0 %collective-permute-start.4 = (bf16[32,2176]{1,0:T(8,128)(2,1)S(1)}, bf16[32,2176]{1,0:T(8,128)(2,1)S(1)}, u32[]{:S(2)}, u32[]{:S(2)}) collective-permute-start(bf16[32,2176]{1,0:T(8,128)(2,1)S(1)} %pad_maximum_fusion.after_ref), channel_id=1, source_target_pairs={{0,4},{1,5},{2,6},{3,7},{4,0},{5,1},{6,2},{7,3},{8,12},{9,13},{10,... | collective-permute-start | bytes 417800 | tf_op jit(solution)/shard_map/ppermute | solution.py:41
  16.3 6.0 %collective-permute-start.5 = (bf16[32,2176]{1,0:T(8,128)(2,1)S(1)}, bf16[32,2176]{1,0:T(8,128)(2,1)S(1)}, u32[]{:S(2)}, u32[]{:S(2)}) collective-permute-start(bf16[32,2176]{1,0:T(8,128)(2,1)S(1)} %pad_maximum_fusion.after_ref), channel_id=1, source_target_pairs={{0,5},{1,4},{2,7},{3,6},{4,1},{5,0},{6,3},{7,2},{8,13},{9,12},{10,... | collective-permute-start | bytes 417800 | tf_op jit(solution)/shard_map/ppermute | solution.py:41
  22.2 4.9 %collective-permute-start.6 = (bf16[128,2176]{1,0:T(8,128)(2,1)S(1)}, bf16[128,2176]{1,0:T(8,128)(2,1)S(1)}, u32[]{:S(2)}, u32[]{:S(2)}) collective-permute-start(bf16[128,2176]{1,0:T(8,128)(2,1)S(1)} %constant_dynamic-update-slice_fusion.buf_ref.refs_0_), channel_id=1, source_target_pairs={{0,2},{1,3},{2,0},{3,1},{4,6},{5,7},{6,4},{7,5},{8,10},{9,11},{10,... | collective-permute-start | bytes 1671176 | tf_op jit(solution)/shard_map/ppermute | solution.py:41
  27.1 17.5 %copy-start = (bf16[2048,16]{0,1:T(8,128)(2,1)S(1)}, bf16[2048,16]{0,1:T(8,128)(2,1)}, u32[]{:S(2)}) copy-start(bf16[2048,16]{0,1:T(8,128)(2,1)} %param.12) | copy-start | bytes 196612
  29.5 1.7 %collective-permute-start.7 = (bf16[64,2176]{1,0:T(8,128)(2,1)S(1)}, bf16[64,2176]{1,0:T(8,128)(2,1)S(1)}, u32[]{:S(2)}, u32[]{:S(2)}) collective-permute-start(bf16[64,2176]{1,0:T(8,128)(2,1)S(1)} %get-tuple-element.27), channel_id=1, source_target_pairs={{0,2},{1,3},{2,0},{3,1},{4,6},{5,7},{6,4},{7,5},{8,10},{9,11},{10,... | collective-permute-start | bytes 835592 | tf_op jit(solution)/shard_map/ppermute | solution.py:41
  31.3 4.6 %collective-permute-start.8 = (bf16[16,2176]{1,0:T(8,128)(2,1)S(1)}, bf16[16,2176]{1,0:T(8,128)(2,1)S(1)}, u32[]{:S(2)}, u32[]{:S(2)}) collective-permute-start(bf16[16,2176]{1,0:T(8,128)(2,1)S(1)} %get-tuple-element.30), channel_id=1, source_target_pairs={{0,1},{1,0},{2,3},{3,2},{4,5},{5,4},{6,7},{7,6},{8,9},{9,8},{10,11... | collective-permute-start | bytes 208904 | tf_op jit(solution)/shard_map/ppermute | solution.py:41
  31.9 4.6 %collective-permute-start.9 = (bf16[16,2176]{1,0:T(8,128)(2,1)S(1)}, bf16[16,2176]{1,0:T(8,128)(2,1)S(1)}, u32[]{:S(2)}, u32[]{:S(2)}) collective-permute-start(bf16[16,2176]{1,0:T(8,128)(2,1)S(1)} %get-tuple-element.31), channel_id=1, source_target_pairs={{0,4},{1,5},{2,6},{3,7},{4,0},{5,1},{6,2},{7,3},{8,12},{9,13},{10,... | collective-permute-start | bytes 208904 | tf_op jit(solution)/shard_map/ppermute | solution.py:41
  32.5 5.2 %collective-permute-start.10 = (bf16[16,2176]{1,0:T(8,128)(2,1)S(1)}, bf16[16,2176]{1,0:T(8,128)(2,1)S(1)}, u32[]{:S(2)}, u32[]{:S(2)}) collective-permute-start(bf16[16,2176]{1,0:T(8,128)(2,1)S(1)} %get-tuple-element.32), channel_id=1, source_target_pairs={{0,5},{1,4},{2,7},{3,6},{4,1},{5,0},{6,3},{7,2},{8,13},{9,12},{10,... | collective-permute-start | bytes 208904 | tf_op jit(solution)/shard_map/ppermute | solution.py:41
  37.8 4.5 %collective-permute-start.11 = (bf16[4,2560]{1,0:T(4,128)(2,1)S(1)}, bf16[4,2560]{1,0:T(4,128)(2,1)S(1)}, u32[]{:S(2)}, u32[]{:S(2)}) collective-permute-start(bf16[4,2560]{1,0:T(4,128)(2,1)S(1)} %get-tuple-element.35), channel_id=1, source_target_pairs={{0,8},{1,9},{2,10},{3,11},{4,12},{5,13},{6,14},{7,15},{8,0},{9,1},... | collective-permute-start | bytes 61448 | tf_op jit(solution)/shard_map/ppermute | solution.py:41
  37.9 4.8 %collective-permute-start.12 = (bf16[4,2560]{1,0:T(4,128)(2,1)S(1)}, bf16[4,2560]{1,0:T(4,128)(2,1)S(1)}, u32[]{:S(2)}, u32[]{:S(2)}) collective-permute-start(bf16[4,2560]{1,0:T(4,128)(2,1)S(1)} %get-tuple-element.36), channel_id=1, source_target_pairs={{0,16},{1,17},{2,18},{3,19},{4,20},{5,21},{6,22},{7,23},{8,24},{9,... | collective-permute-start | bytes 61448 | tf_op jit(solution)/shard_map/ppermute | solution.py:41
  39.0 5.6 %collective-permute-start.13 = (bf16[4,2560]{1,0:T(4,128)(2,1)S(1)}, bf16[4,2560]{1,0:T(4,128)(2,1)S(1)}, u32[]{:S(2)}, u32[]{:S(2)}) collective-permute-start(bf16[4,2560]{1,0:T(4,128)(2,1)S(1)} %get-tuple-element.37), channel_id=1, source_target_pairs={{0,24},{1,25},{2,26},{3,27},{4,28},{5,29},{6,30},{7,31},{8,16},{9,... | collective-permute-start | bytes 61448 | tf_op jit(solution)/shard_map/ppermute | solution.py:41
where the time goes:
time: 46 us; the launch traced here: 45.9 us
  starting transfers between devices  17.9 us (39%)
  waiting for transfers between devices  17.5 us (38%)
  Pallas kernels  9.62 us (21%)
  between operations  0.72 us (2%)
    ppermute x14, starting transfers between devices, swap(): return lax.ppermute(block, AXES, [(i, i ^ mask) for i in range(count)])  17.9 us
    ppermute x14, waiting for transfers between devices, swap(): return lax.ppermute(block, AXES, [(i, i ^ mask) for i in range(count)])  17.5 us
    pallas_call x1, Pallas kernels, on_device(): pl.pallas_call(functools.partial(load_kernel, chunks), out_shape=tuple((p...  2.41 us
    pallas_call x1, Pallas kernels, on_device(): pl.pallas_call(functools.partial(half_kernel, bits, core_mask, True), out...  2.36 us
    pallas_call x1, Pallas kernels, on_device(): pl.pallas_call(functools.partial(half_kernel, bits, 0, False), out_shape=...  2.35 us
    pallas_call x1, Pallas kernels, on_device(): pl.pallas_call(functools.partial(final_kernel, len(arrived), bits, back_b...  1.25 us
    pallas_call x1, Pallas kernels, on_device(): pl.pallas_call(prep_kernel, out_shape=jax.ShapeDtypeStruct((2 * tok, widt...  1.12 us
  transfers between devices with their start and end apart: 14, of which 11 were waited for; matrix products, arithmetic and copies ran while one was open for 0% of the time, Pallas kernels for 10%

commit v1 on v0

--- a/solution.py
+++ b/solution.py
@@ -27,13 +27,14 @@
     first = list(range(max(core + 1, all_bits - 2), all_bits))
     middle = [b for b in range(all_bits) if b != core and b not in first]
     groups = [first] + [middle[i : i + 2] for i in range(0, len(middle), 2)]
-    return groups, core
-
-
-def group_masks(bits):
+    bases = [[sum(1 << b for b in group[i:]) for i in range(len(group))] for group in groups]
+    return bases, 1 << core
+
+
+def group_masks(basis):
     masks = [0]
-    for bit in bits:
-        masks = masks + [m | (1 << bit) for m in masks]
+    for mask in basis:
+        masks = masks + [m ^ mask for m in masks]
     return masks
 
 
@@ -41,10 +42,10 @@
     return lax.ppermute(block, AXES, [(i, i ^ mask) for i in range(count)])
 
 
-def place_mask(place, bits):
+def place_mask(place, basis):
     total = jnp.zeros_like(place)
-    for digit, bit in enumerate(bits):
-        total = total | (((place >> digit) & 1) << bit)
+    for digit, mask in enumerate(basis):
+        total = total ^ (((place >> digit) & 1) * mask)
     return total
 
 
@@ -134,7 +135,7 @@
         scores_ref[base + c * rows : base + c * rows + here, :] = block[:here]
 
 
-def half_kernel(bits, swap_mask, last, buf_ref, gate_ref, up_ref, down_ref, *rest):
+def half_kernel(basis, swap_mask, last, buf_ref, gate_ref, up_ref, down_ref, *rest):
     width = gate_ref.shape[1]
     experts_width = buf_ref.shape[1] - width
     own = own_index()
@@ -182,7 +183,7 @@
 
         row = lax.broadcasted_iota(jnp.int32, (step, tokens), 0) + start
         token = lax.broadcasted_iota(jnp.int32, (step, tokens), 1)
-        whole = (place_mask(row >> 3, bits) ^ (own ^ swap_mask)) * 4 + (row & 7)
+        whole = (place_mask(row >> 3, basis) ^ (own ^ swap_mask)) * 4 + (row & 7)
         here = (whole == token) & ((row & 7) < 4)
         score_ref[...] += jnp.sum(jnp.where(here, score, 0.0), axis=0, keepdims=True)
 
@@ -229,59 +230,65 @@
         put_scores(ref, scores_ref, width)
 
 
-def final_kernel(arrivals, bits, back_bits, core_mask, *refs):
-    buf_own_ref, buf_other_ref, router_ref, kept_ref, pieces_ref = refs[:5]
-    arrived = refs[5 : 5 + arrivals]
-    x_ref, grad_ref, scores_ref, lg_ref = refs[5 + arrivals :]
+def table_kernel(basis, core_mask, rows_out, after_ref, buf_own_ref, buf_other_ref, here_ref, probs_ref, column_ref):
+    half, buf_width = buf_own_ref.shape
+    experts = probs_ref.shape[1]
+    tokens = here_ref.shape[1]
+    width = buf_width - -(-PIECES * experts // LANES) * LANES
+    lanes = buf_width - width
+    own = own_index()
+    lane = lax.broadcasted_iota(jnp.int32, (lanes, experts), 0)
+    ids = lax.broadcasted_iota(jnp.int32, (lanes, experts), 1)
+    tally = jnp.zeros((lanes, experts), F32)
+    for k in range(1, PIECES):
+        tally = tally + jnp.where(lane == ids + k * experts, 1.0, 0.0)
+    column = pl.multiple_of(own * rows_out // LANES * LANES, LANES)
+    for index, ref in enumerate((buf_own_ref, buf_other_ref)):
+        row = lax.broadcasted_iota(jnp.int32, (half, tokens), 0)
+        token = lax.broadcasted_iota(jnp.int32, (half, tokens), 1)
+        whole = (place_mask(row >> 3, basis) ^ (own ^ (core_mask if index else 0))) * 4 + (row & 7)
+        here = jnp.where((whole == token) & ((row & 7) < 4), 1.0, 0.0).astype(BF16)
+        part = slice(index * half, (index + 1) * half)
+        here_ref[part, :] = here
+        probs_ref[part, :] = jnp.dot(ref[:, width:], tally.astype(BF16), preferred_element_type=F32)
+        column_ref[part, :] = ref[:, pl.ds(column, LANES)]
+
+
+def final_kernel(arrivals, back_basis, *refs):
+    here_ref, probs_ref, column_ref, router_ref, kept_ref, pieces_ref = refs[:6]
+    arrived = refs[6 : 6 + arrivals]
+    x_ref, grad_ref, scores_ref = refs[6 + arrivals :]
     experts, width = router_ref.shape
-    half, buf_width = buf_own_ref.shape
-    lanes = buf_width - width
     size = pieces_ref.shape[0]
     tok = kept_ref.shape[0]
     own = own_index()
     scores_ref[0:size, :] = pieces_ref[...]
     for j, ref in enumerate(arrived):
         get_scores(ref, scores_ref, (j + 1) * size, size, width)
-    tokens = half * 2 // 8 * 4
-    blocks = tokens // LANES
+    blocks = here_ref.shape[1] // LANES
     wide = scores_ref.shape[0] // blocks
     sender = lax.broadcasted_iota(jnp.int32, (wide, experts), 0) // SCORE_PIECES
     ids = lax.broadcasted_iota(jnp.int32, (wide, experts), 1)
-    pick = jnp.where(((place_mask(sender, back_bits) ^ own) >> 1) == ids, 1.0, 0.0).astype(BF16)
-    lane = lax.broadcasted_iota(jnp.int32, (lanes, experts), 0)
-    ids = lax.broadcasted_iota(jnp.int32, (lanes, experts), 1)
-    tally = jnp.zeros((lanes, experts), F32)
-    for k in range(1, PIECES):
-        tally = tally + jnp.where(lane == ids + k * experts, 1.0, 0.0)
-    rows_out = grad_ref.shape[1]
-    first = own * rows_out
-    column = pl.multiple_of(first // LANES * LANES, LANES)
-    grad = jnp.zeros((experts, LANES), F32)
-    for index, ref in enumerate((buf_own_ref, buf_other_ref)):
-        picked = jnp.zeros((half, wide), F32)
-        for b in range(blocks):
-            row = lax.broadcasted_iota(jnp.int32, (half, LANES), 0)
-            token = lax.broadcasted_iota(jnp.int32, (half, LANES), 1) + b * LANES
-            whole = (place_mask(row >> 3, bits) ^ (own ^ (core_mask if index else 0))) * 4 + (row & 7)
-            here = jnp.where((whole == token) & ((row & 7) < 4), 1.0, 0.0).astype(BF16)
-            block = scores_ref[...] if blocks == 1 else scores_ref[pl.ds(b, wide, stride=blocks), :]
-            picked = picked + lax.dot_general(here, block.astype(BF16), NT, preferred_element_type=F32)
-        scores = jnp.dot(picked.astype(BF16), pick, preferred_element_type=F32)
-        probs = jnp.dot(ref[:, width:], tally.astype(BF16), preferred_element_type=F32)
-        mean = jnp.sum(probs * scores, axis=1, keepdims=True)
-        logit_grad = probs * (scores - mean)
-        if index == 0:
-            lg_ref[...] = logit_grad[0:8]
-        grad = grad + lax.dot_general(
-            logit_grad.astype(BF16), ref[:, pl.ds(column, LANES)], TN, preferred_element_type=F32
+    pick = jnp.where(((place_mask(sender, back_basis) ^ own) >> 1) == ids, 1.0, 0.0).astype(BF16)
+    picked = jnp.zeros((here_ref.shape[0], wide), F32)
+    for b in range(blocks):
+        block = scores_ref[...] if blocks == 1 else scores_ref[pl.ds(b, wide, stride=blocks), :]
+        picked = picked + lax.dot_general(
+            here_ref[:, b * LANES : (b + 1) * LANES], block.astype(BF16), NT, preferred_element_type=F32
         )
-    shift = (LANES - (first - column)) % LANES
-    grad_ref[...] = pltpu.roll(grad, shift, 1)[:, :rows_out]
-    part = jnp.dot(lg_ref[...].astype(BF16), router_ref[...], preferred_element_type=F32)
+    scores = jnp.dot(picked.astype(BF16), pick, preferred_element_type=F32)
+    probs = probs_ref[...]
+    mean = jnp.sum(probs * scores, axis=1, keepdims=True)
+    logit_grad = (probs * (scores - mean)).astype(BF16)
+    part = jnp.dot(logit_grad[0:16], router_ref[...], preferred_element_type=F32)
     total = kept_ref[...]
     for ref in arrived:
         total = total + ref[:, 0:width].astype(F32)
     x_ref[...] = (total + part[:tok]).astype(BF16)
+    grad = lax.dot_general(logit_grad, column_ref[...], TN, preferred_element_type=F32)
+    rows_out = grad_ref.shape[1]
+    first = own * rows_out % LANES
+    grad_ref[...] = pltpu.roll(grad, (LANES - first) % LANES, 1)[:, :rows_out]
 
 
 def on_device(tokens, grad_out, router_logits, selected, router_w, w_gate, w_up, w_down):
@@ -292,11 +299,9 @@
     hid_size = lax.axis_size("hid")
     count = exp_size * hid_size
     half = count // 2
-    groups, core = stage_masks(exp_size, hid_size)
-    core_mask = 1 << core
-    bits = [b for group in groups for b in group]
-    back_groups = [[core]] + groups[::-1]
-    back_bits = [b for group in back_groups for b in group]
+    groups, core_mask = stage_masks(exp_size, hid_size)
+    basis = [m for group in groups for m in group]
+    back_basis = [core_mask] + [m for group in groups[::-1] for m in group]
     token_count = count * tok
     lanes = -(-PIECES * experts // LANES) * LANES
 
@@ -341,7 +346,7 @@
     )
     unit_rows = SCORE_PIECES * token_count // LANES
     kept, score = pl.pallas_call(
-        functools.partial(half_kernel, bits, 0, False),
+        functools.partial(half_kernel, basis, 0, False),
         out_shape=(
             jax.ShapeDtypeStruct((half * tok, width), F32),
             jax.ShapeDtypeStruct((1, token_count), F32),
@@ -349,12 +354,14 @@
         in_specs=[VMEM_SPEC] * 4,
         out_specs=(VMEM_SPEC, VMEM_SPEC),
         compiler_params=PARAMS,
-        cost_estimate=cost,
+        cost_estimate=pl.CostEstimate(
+            flops=cost.flops * 16, bytes_accessed=cost.bytes_accessed, transcendentals=cost.transcendentals
+        ),
         name="half_own",
     )(block, *weights)
     extra = -(-unit_rows // (half * tok)) * LANES
     message, pieces = pl.pallas_call(
-        functools.partial(half_kernel, bits, core_mask, True),
+        functools.partial(half_kernel, basis, core_mask, True),
         out_shape=(
             jax.ShapeDtypeStruct((half * tok, width + extra), BF16),
             jax.ShapeDtypeStruct((unit_rows, LANES), F32),
@@ -371,6 +378,8 @@
     )(other, *weights, score)
 
     arrived = [swap(message, core_mask, count)]
+    tables = None
+    rows_out = width // count
     for group in groups[::-1]:
         masks = group_masks(group)
         radix = len(masks)
@@ -396,23 +405,34 @@
             name="add",
         )(kept, pieces, *arrived)
         kept, pieces = outs[0], outs[1]
+        if tables is None:
+            tables = pl.pallas_call(
+                functools.partial(table_kernel, basis, core_mask, rows_out),
+                out_shape=(
+                    jax.ShapeDtypeStruct((2 * block.shape[0], token_count), BF16),
+                    jax.ShapeDtypeStruct((2 * block.shape[0], experts), F32),
+                    jax.ShapeDtypeStruct((2 * block.shape[0], LANES), BF16),
+                ),
+                in_specs=[pl.BlockSpec(memory_space=pl.ANY)] + [VMEM_SPEC] * 2,
+                out_specs=(VMEM_SPEC,) * 3,
+                compiler_params=PARAMS,
+                cost_estimate=pl.CostEstimate(flops=10**9, bytes_accessed=10**6, transcendentals=0),
+                name="tables",
+            )(pieces, block, other)
         arrived = [swap(piece, m, count) for piece, m in zip(outs[2:], masks[1:])]
 
     x_grad, grad = pl.pallas_call(
-        functools.partial(final_kernel, len(arrived), bits, back_bits, core_mask),
+        functools.partial(final_kernel, len(arrived), back_basis),
         out_shape=(
             jax.ShapeDtypeStruct((tok, width), BF16),
-            jax.ShapeDtypeStruct((experts, width // count), F32),
+            jax.ShapeDtypeStruct((experts, rows_out), F32),
         ),
-        in_specs=[VMEM_SPEC] * (5 + len(arrived)),
+        in_specs=[VMEM_SPEC] * (6 + len(arrived)),
         out_specs=(VMEM_SPEC, VMEM_SPEC),
-        scratch_shapes=[
-            pltpu.VMEM((pieces.shape[0] * (1 + len(arrived)), LANES), F32),
-            pltpu.VMEM((8, experts), F32),
-        ],
+        scratch_shapes=[pltpu.VMEM((pieces.shape[0] * (1 + len(arrived)), LANES), F32)],
         compiler_params=PARAMS,
         name="final",
-    )(block, other, router_w.T, kept, pieces, *arrived)
+    )(*tables, router_w.T, kept, pieces, *arrived)
     return (x_grad, grad.T)
 
 

time: 46 us -> 41.8 us (0.909)
  waiting for transfers between devices: 17.5 us -> 13.1 us
    ppermute x14, waiting for transfers between devices: 17.5 us -> 13.1 us  [swap(): return lax.ppermute(block, AXES, [(i, i ^ mask) for i in range(count)])]
    pallas_call x3 -> x4, Pallas kernels: 5.95 us -> 6.12 us  [the longest x1 2.36 us: on_device(): pl.pallas_call(functools.partial(half_kernel, basis, 0, False), out_shape...]
  transfers between devices with their start and end apart: 14 -> 14, of which waited for: 11 -> 10; matrix products, arithmetic and copies ran while one was open for 0% -> 0% of each run, Pallas kernels for 10% -> 12%
where the time goes in v1:
time: 41.8 us; the launch traced here: 41.7 us
  starting transfers between devices  18 us (43%)
  waiting for transfers between devices  13.1 us (31%)
  Pallas kernels  9.78 us (23%)
  between operations  0.72 us (2%)
    ppermute x14, starting transfers between devices, swap(): return lax.ppermute(block, AXES, [(i, i ^ mask) for i in range(count)])  18 us
    ppermute x14, waiting for transfers between devices, swap(): return lax.ppermute(block, AXES, [(i, i ^ mask) for i in range(count)])  13.1 us
    pallas_call x1, Pallas kernels, on_device(): pl.pallas_call(functools.partial(load_kernel, chunks), out_shape=tuple((p...  2.41 us
    pallas_call x1, Pallas kernels, on_device(): pl.pallas_call(functools.partial(half_kernel, basis, 0, False), out_shape...  2.36 us
    pallas_call x1, Pallas kernels, on_device(): pl.pallas_call(functools.partial(half_kernel, basis, core_mask, True), ou...  2.35 us
    pallas_call x1, Pallas kernels, on_device(): pl.pallas_call(functools.partial(final_kernel, len(arrived), back_basis),...  1.2 us
    pallas_call x1, Pallas kernels, on_device(): pl.pallas_call(prep_kernel, out_shape=jax.ShapeDtypeStruct((2 * tok, widt...  1.12 us
  transfers between devices with their start and end apart: 14, of which 10 were waited for; matrix products, arithmetic and copies ran while one was open for 0% of the time, Pallas kernels for 12%

profile of v1, /device:TPU:0, one launch (start us, length us, event | category | flops | bytes accessed | tf_op | source)
XLA Modules:
  0.0 41.7 jit_solution(11201330494215789656)
XLA Ops:
  0.6 1.1 %prep.1 = bf16[8,2176]{1,0:T(8,128)(2,1)S(1)} custom-call(bf16[4,2048]{1,0:T(4,128)(2,1)} %tokens_in.1, bf16[4,2048]{1,0:T(4,128)(2,1)} %grad_in.1, f32[4,16]{1,0:T(4,128)} %logits_in.1, s32[4,8]{1,0:T(4,128)} %chosen_in.1), custom_call_target="tpu_custom_call" | custom-call | tf_op jit(solution)/shard_map/prep/pallas_call | solution.py:308
  1.8 5.1 %collective-permute-start = (bf16[8,2176]{1,0:T(8,128)(2,1)S(1)}, bf16[8,2176]{1,0:T(8,128)(2,1)S(1)}, u32[]{:S(2)}, u32[]{:S(2)}) collective-permute-start(bf16[8,2176]{1,0:T(8,128)(2,1)S(1)} %prep.1), channel_id=1, source_target_pairs={{0,24},{1,25},{2,26},{3,27},{4,28},{5,29},{6,30},{7,31},{8,16},{9,... | collective-permute-start | bytes 104456 | tf_op jit(solution)/shard_map/ppermute | solution.py:42
  6.9 0.0 collective-permute-start.1
  6.9 0.6 %collective-permute-start.2 = (bf16[8,2176]{1,0:T(8,128)(2,1)S(1)}, bf16[8,2176]{1,0:T(8,128)(2,1)S(1)}, u32[]{:S(2)}, u32[]{:S(2)}) collective-permute-start(bf16[8,2176]{1,0:T(8,128)(2,1)S(1)} %prep.1), channel_id=1, source_target_pairs={{0,8},{1,9},{2,10},{3,11},{4,12},{5,13},{6,14},{7,15},{8,0},{9,1},... | collective-permute-start | bytes 104456 | tf_op jit(solution)/shard_map/ppermute | solution.py:42
  7.5 1.3 %collective-permute-done = bf16[8,2176]{1,0:T(8,128)(2,1)S(1)} collective-permute-done((bf16[8,2176]{1,0:T(8,128)(2,1)S(1)}, bf16[8,2176]{1,0:T(8,128)(2,1)S(1)}, u32[]{:S(2)}, u32[]{:S(2)}) %collective-permute-start) | collective-permute-done | bytes 34848 | tf_op jit(solution)/shard_map/ppermute | solution.py:42
  8.8 2.9 %collective-permute-done.1 = bf16[8,2176]{1,0:T(8,128)(2,1)S(1)} collective-permute-done((bf16[8,2176]{1,0:T(8,128)(2,1)S(1)}, bf16[8,2176]{1,0:T(8,128)(2,1)S(1)}, u32[]{:S(2)}, u32[]{:S(2)}) %collective-permute-start.1) | collective-permute-done | bytes 34848 | tf_op jit(solution)/shard_map/ppermute | solution.py:42
  11.7 2.5 %collective-permute-start.3 = (bf16[32,2176]{1,0:T(8,128)(2,1)S(1)}, bf16[32,2176]{1,0:T(8,128)(2,1)S(1)}, u32[]{:S(2)}, u32[]{:S(2)}) collective-permute-start(bf16[32,2176]{1,0:T(8,128)(2,1)S(1)} %pad_maximum_fusion.after_ref), channel_id=1, source_target_pairs={{0,5},{1,4},{2,7},{3,6},{4,1},{5,0},{6,3},{7,2},{8,13},{9,12},{10,... | collective-permute-start | bytes 417800 | tf_op jit(solution)/shard_map/ppermute | solution.py:42
  14.2 0.5 %collective-permute-start.4 = (bf16[32,2176]{1,0:T(8,128)(2,1)S(1)}, bf16[32,2176]{1,0:T(8,128)(2,1)S(1)}, u32[]{:S(2)}, u32[]{:S(2)}) collective-permute-start(bf16[32,2176]{1,0:T(8,128)(2,1)S(1)} %pad_maximum_fusion.after_ref), channel_id=1, source_target_pairs={{0,4},{1,5},{2,6},{3,7},{4,0},{5,1},{6,2},{7,3},{8,12},{9,13},{10,... | collective-permute-start | bytes 417800 | tf_op jit(solution)/shard_map/ppermute | solution.py:42
  14.7 0.5 %collective-permute-start.5 = (bf16[32,2176]{1,0:T(8,128)(2,1)S(1)}, bf16[32,2176]{1,0:T(8,128)(2,1)S(1)}, u32[]{:S(2)}, u32[]{:S(2)}) collective-permute-start(bf16[32,2176]{1,0:T(8,128)(2,1)S(1)} %pad_maximum_fusion.after_ref), channel_id=1, source_target_pairs={{0,1},{1,0},{2,3},{3,2},{4,5},{5,4},{6,7},{7,6},{8,9},{9,8},{10,11... | collective-permute-start | bytes 417800 | tf_op jit(solution)/shard_map/ppermute | solution.py:42
  15.3 2.4 %load.1 = (bf16[1,2048,384]{2,1,0:T(8,128)(2,1)S(1)}, bf16[1,2048,384]{2,1,0:T(8,128)(2,1)S(1)}, bf16[1,384,2048]{2,1,0:T(8,128)(2,1)S(1)}) custom-call(bf16[32,2176]{1,0:T(8,128)(2,1)S(1)} %pad_maximum_fusion.after_ref, bf16[1,2048,384]{2,1,0:T(8,128)(2,1)} %refs_0_.1, bf16[1,2048,384]{2,1,0:T(8,128)(2,1)} %refs_1_.1, bf16[1,384,2048]{2,1,0:T(8,128)(2,1)} %refs_2_.1), custom_call_target="tpu_custom_call" | custom-call | bytes 9437184 | tf_op jit(solution)/shard_map/load/pallas_call | solution.py:329
  17.7 1.5 %collective-permute-done.3 = bf16[32,2176]{1,0:T(8,128)(2,1)S(1)} collective-permute-done((bf16[32,2176]{1,0:T(8,128)(2,1)S(1)}, bf16[32,2176]{1,0:T(8,128)(2,1)S(1)}, u32[]{:S(2)}, u32[]{:S(2)}) %collective-permute-start.3) | collective-permute-done | bytes 139296 | tf_op jit(solution)/shard_map/ppermute | solution.py:42
  19.3 0.8 %collective-permute-done.4 = bf16[32,2176]{1,0:T(8,128)(2,1)S(1)} collective-permute-done((bf16[32,2176]{1,0:T(8,128)(2,1)S(1)}, bf16[32,2176]{1,0:T(8,128)(2,1)S(1)}, u32[]{:S(2)}, u32[]{:S(2)}) %collective-permute-start.4) | collective-permute-done | bytes 139296 | tf_op jit(solution)/shard_map/ppermute | solution.py:42
  20.1 0.1 collective-permute-start.6
  20.1 2.4 %half_own.1 = (f32[64,2048]{1,0:T(8,128)S(1)}, f32[1,128]{1,0:T(1,128)S(1)}) custom-call(bf16[128,2176]{1,0:T(8,128)(2,1)S(1)} %constant_dynamic-update-slice_fusion.buf_ref.buf_own_ref, bf16[1,2048,384]{2,1,0:T(8,128)(2,1)S(1)} %get-tuple-element.24.gate_ref, bf16[1,2048,384]{2,1,0:T(8,128)(2,1)S(1)} %get-tuple-element.25.up_ref, ...), custom_call_target="tpu_custom_call" | custom-call | flops 12884901888 | bytes 5242880 | tf_op jit(solution)/shard_map/half_own/pallas_call | solution.py:348
  22.5 2.4 %half_other.1 = (bf16[64,2176]{1,0:T(8,128)(2,1)S(1)}, f32[2,128]{1,0:T(2,128)S(1)}) custom-call(bf16[128,2176]{1,0:T(8,128)(2,1)S(1)} %collective-permute-done.6.buf_ref.buf_other_ref, bf16[1,2048,384]{2,1,0:T(8,128)(2,1)S(1)} %get-tuple-element.24.gate_ref, bf16[1,2048,384]{2,1,0:T(8,128)(2,1)S(1)} %get-tuple-element.25.up_ref, ...), custom_call_target="tpu_custom_call" | custom-call | flops 805306368 | bytes 5242880 | tf_op jit(solution)/shard_map/half_other/pallas_call | solution.py:363
  24.9 0.6 %collective-permute-start.7 = (bf16[64,2176]{1,0:T(8,128)(2,1)S(1)}, bf16[64,2176]{1,0:T(8,128)(2,1)S(1)}, u32[]{:S(2)}, u32[]{:S(2)}) collective-permute-start(bf16[64,2176]{1,0:T(8,128)(2,1)S(1)} %get-tuple-element.30), channel_id=1, source_target_pairs={{0,2},{1,3},{2,0},{3,1},{4,6},{5,7},{6,4},{7,5},{8,10},{9,11},{10,... | collective-permute-start | bytes 835592 | tf_op jit(solution)/shard_map/ppermute | solution.py:42
  25.4 1.2 %collective-permute-done.7.refs_2_ = bf16[64,2176]{1,0:T(8,128)(2,1)S(1)} collective-permute-done((bf16[64,2176]{1,0:T(8,128)(2,1)S(1)}, bf16[64,2176]{1,0:T(8,128)(2,1)S(1)}, u32[]{:S(2)}, u32[]{:S(2)}) %collective-permute-start.7) | collective-permute-done | bytes 278560 | tf_op jit(solution)/shard_map/ppermute | solution.py:42
  26.6 0.1 add.2
  26.7 1.5 %collective-permute-start.8 = (bf16[16,2176]{1,0:T(8,128)(2,1)S(1)}, bf16[16,2176]{1,0:T(8,128)(2,1)S(1)}, u32[]{:S(2)}, u32[]{:S(2)}) collective-permute-start(bf16[16,2176]{1,0:T(8,128)(2,1)S(1)} %get-tuple-element.36), channel_id=1, source_target_pairs={{0,5},{1,4},{2,7},{3,6},{4,1},{5,0},{6,3},{7,2},{8,13},{9,12},{10,... | collective-permute-start | bytes 208904 | tf_op jit(solution)/shard_map/ppermute | solution.py:42
  28.2 1.3 %collective-permute-start.9 = (bf16[16,2176]{1,0:T(8,128)(2,1)S(1)}, bf16[16,2176]{1,0:T(8,128)(2,1)S(1)}, u32[]{:S(2)}, u32[]{:S(2)}) collective-permute-start(bf16[16,2176]{1,0:T(8,128)(2,1)S(1)} %get-tuple-element.37), channel_id=1, source_target_pairs={{0,4},{1,5},{2,6},{3,7},{4,0},{5,1},{6,2},{7,3},{8,12},{9,13},{10,... | collective-permute-start | bytes 208904 | tf_op jit(solution)/shard_map/ppermute | solution.py:42
  29.5 0.8 %collective-permute-start.10 = (bf16[16,2176]{1,0:T(8,128)(2,1)S(1)}, bf16[16,2176]{1,0:T(8,128)(2,1)S(1)}, u32[]{:S(2)}, u32[]{:S(2)}) collective-permute-start(bf16[16,2176]{1,0:T(8,128)(2,1)S(1)} %get-tuple-element.38), channel_id=1, source_target_pairs={{0,1},{1,0},{2,3},{3,2},{4,5},{5,4},{6,7},{7,6},{8,9},{9,8},{10,11... | collective-permute-start | bytes 208904 | tf_op jit(solution)/shard_map/ppermute | solution.py:42
  30.3 2.0 %collective-permute-done.8.refs_2_ = bf16[16,2176]{1,0:T(8,128)(2,1)S(1)} collective-permute-done((bf16[16,2176]{1,0:T(8,128)(2,1)S(1)}, bf16[16,2176]{1,0:T(8,128)(2,1)S(1)}, u32[]{:S(2)}, u32[]{:S(2)}) %collective-permute-start.8) | collective-permute-done | bytes 69664 | tf_op jit(solution)/shard_map/ppermute | solution.py:42
  32.3 1.4 %collective-permute-done.9.refs_3_ = bf16[16,2176]{1,0:T(8,128)(2,1)S(1)} collective-permute-done((bf16[16,2176]{1,0:T(8,128)(2,1)S(1)}, bf16[16,2176]{1,0:T(8,128)(2,1)S(1)}, u32[]{:S(2)}, u32[]{:S(2)}) %collective-permute-start.9) | collective-permute-done | bytes 69664 | tf_op jit(solution)/shard_map/ppermute | solution.py:42
  33.6 0.2 collective-permute-done.10.refs_4_
  33.8 0.1 add.3
  33.9 1.9 %collective-permute-start.11 = (bf16[4,2560]{1,0:T(4,128)(2,1)S(1)}, bf16[4,2560]{1,0:T(4,128)(2,1)S(1)}, u32[]{:S(2)}, u32[]{:S(2)}) collective-permute-start(bf16[4,2560]{1,0:T(4,128)(2,1)S(1)} %get-tuple-element.41), channel_id=1, source_target_pairs={{0,24},{1,25},{2,26},{3,27},{4,28},{5,29},{6,30},{7,31},{8,16},{9,... | collective-permute-start | bytes 61448 | tf_op jit(solution)/shard_map/ppermute | solution.py:42
  35.8 0.3 collective-permute-start.12
  36.1 2.3 %collective-permute-start.13 = (bf16[4,2560]{1,0:T(4,128)(2,1)S(1)}, bf16[4,2560]{1,0:T(4,128)(2,1)S(1)}, u32[]{:S(2)}, u32[]{:S(2)}) collective-permute-start(bf16[4,2560]{1,0:T(4,128)(2,1)S(1)} %get-tuple-element.43), channel_id=1, source_target_pairs={{0,8},{1,9},{2,10},{3,11},{4,12},{5,13},{6,14},{7,15},{8,0},{9,1},... | collective-permute-start | bytes 61448 | tf_op jit(solution)/shard_map/ppermute | solution.py:42
  38.3 0.2 tables.1
  38.5 1.0 %collective-permute-done.11.refs_6_ = bf16[4,2560]{1,0:T(4,128)(2,1)S(1)} collective-permute-done((bf16[4,2560]{1,0:T(4,128)(2,1)S(1)}, bf16[4,2560]{1,0:T(4,128)(2,1)S(1)}, u32[]{:S(2)}, u32[]{:S(2)}) %collective-permute-start.11) | collective-permute-done | bytes 20512 | tf_op jit(solution)/shard_map/ppermute | solution.py:42
  39.5 0.9 %collective-permute-done.12.refs_7_ = bf16[4,2560]{1,0:T(4,128)(2,1)S(1)} collective-permute-done((bf16[4,2560]{1,0:T(4,128)(2,1)S(1)}, bf16[4,2560]{1,0:T(4,128)(2,1)S(1)}, u32[]{:S(2)}, u32[]{:S(2)}) %collective-permute-start.12) | collective-permute-done | bytes 20512 | tf_op jit(solution)/shard_map/ppermute | solution.py:42
  40.5 1.2 %final.1 = (bf16[4,2048]{1,0:T(4,128)(2,1)}, f32[16,64]{1,0:T(8,128)}) custom-call(bf16[256,128]{1,0:T(8,128)(2,1)S(1)} %get-tuple-element.32.refs_0_, f32[256,16]{1,0:T(8,128)S(1)} %get-tuple-element.33.refs_1_, bf16[256,128]{1,0:T(8,128)(2,1)S(1)} %get-tuple-element.34.refs_2_, bf16[16,2048]{1,0:T(8,128)(2,1)S(1)} %bitcast.2, ...), custom_call_target="tpu_custom_call" | custom-call | tf_op jit(solution)/shard_map/final/pallas_call | solution.py:424
  (14 shorter events, 0.1 us)
Async XLA Ops:
  1.8 7.0 %collective-permute-start = (bf16[8,2176]{1,0:T(8,128)(2,1)S(1)}, bf16[8,2176]{1,0:T(8,128)(2,1)S(1)}, u32[]{:S(2)}, u32[]{:S(2)}) collective-permute-start(bf16[8,2176]{1,0:T(8,128)(2,1)S(1)} %prep.1), channel_id=1, source_target_pairs={{0,24},{1,25},{2,26},{3,27},{4,28},{5,29},{6,30},{7,31},{8,16},{9,... | collective-permute-start | bytes 104456 | tf_op jit(solution)/shard_map/ppermute | solution.py:42
  6.9 4.8 %collective-permute-start.1 = (bf16[8,2176]{1,0:T(8,128)(2,1)S(1)}, bf16[8,2176]{1,0:T(8,128)(2,1)S(1)}, u32[]{:S(2)}, u32[]{:S(2)}) collective-permute-start(bf16[8,2176]{1,0:T(8,128)(2,1)S(1)} %prep.1), channel_id=1, source_target_pairs={{0,16},{1,17},{2,18},{3,19},{4,20},{5,21},{6,22},{7,23},{8,24},{9,... | collective-permute-start | bytes 104456 | tf_op jit(solution)/shard_map/ppermute | solution.py:42
  6.9 4.8 %collective-permute-start.2 = (bf16[8,2176]{1,0:T(8,128)(2,1)S(1)}, bf16[8,2176]{1,0:T(8,128)(2,1)S(1)}, u32[]{:S(2)}, u32[]{:S(2)}) collective-permute-start(bf16[8,2176]{1,0:T(8,128)(2,1)S(1)} %prep.1), channel_id=1, source_target_pairs={{0,8},{1,9},{2,10},{3,11},{4,12},{5,13},{6,14},{7,15},{8,0},{9,1},... | collective-permute-start | bytes 104456 | tf_op jit(solution)/shard_map/ppermute | solution.py:42
  11.7 7.5 %collective-permute-start.3 = (bf16[32,2176]{1,0:T(8,128)(2,1)S(1)}, bf16[32,2176]{1,0:T(8,128)(2,1)S(1)}, u32[]{:S(2)}, u32[]{:S(2)}) collective-permute-start(bf16[32,2176]{1,0:T(8,128)(2,1)S(1)} %pad_maximum_fusion.after_ref), channel_id=1, source_target_pairs={{0,5},{1,4},{2,7},{3,6},{4,1},{5,0},{6,3},{7,2},{8,13},{9,12},{10,... | collective-permute-start | bytes 417800 | tf_op jit(solution)/shard_map/ppermute | solution.py:42
  14.2 5.8 %collective-permute-start.4 = (bf16[32,2176]{1,0:T(8,128)(2,1)S(1)}, bf16[32,2176]{1,0:T(8,128)(2,1)S(1)}, u32[]{:S(2)}, u32[]{:S(2)}) collective-permute-start(bf16[32,2176]{1,0:T(8,128)(2,1)S(1)} %pad_maximum_fusion.after_ref), channel_id=1, source_target_pairs={{0,4},{1,5},{2,6},{3,7},{4,0},{5,1},{6,2},{7,3},{8,12},{9,13},{10,... | collective-permute-start | bytes 417800 | tf_op jit(solution)/shard_map/ppermute | solution.py:42
  14.7 5.3 %collective-permute-start.5 = (bf16[32,2176]{1,0:T(8,128)(2,1)S(1)}, bf16[32,2176]{1,0:T(8,128)(2,1)S(1)}, u32[]{:S(2)}, u32[]{:S(2)}) collective-permute-start(bf16[32,2176]{1,0:T(8,128)(2,1)S(1)} %pad_maximum_fusion.after_ref), channel_id=1, source_target_pairs={{0,1},{1,0},{2,3},{3,2},{4,5},{5,4},{6,7},{7,6},{8,9},{9,8},{10,11... | collective-permute-start | bytes 417800 | tf_op jit(solution)/shard_map/ppermute | solution.py:42
  20.1 2.5 %collective-permute-start.6 = (bf16[128,2176]{1,0:T(8,128)(2,1)S(1)}, bf16[128,2176]{1,0:T(8,128)(2,1)S(1)}, u32[]{:S(2)}, u32[]{:S(2)}) collective-permute-start(bf16[128,2176]{1,0:T(8,128)(2,1)S(1)} %constant_dynamic-update-slice_fusion.buf_ref.buf_own_ref), channel_id=1, source_target_pairs={{0,2},{1,3},{2,0},{3,1},{4,6},{5,7},{6,4},{7,5},{8,10},{9,11},{10,... | collective-permute-start | bytes 1671176 | tf_op jit(solution)/shard_map/ppermute | solution.py:42
  24.9 1.7 %collective-permute-start.7 = (bf16[64,2176]{1,0:T(8,128)(2,1)S(1)}, bf16[64,2176]{1,0:T(8,128)(2,1)S(1)}, u32[]{:S(2)}, u32[]{:S(2)}) collective-permute-start(bf16[64,2176]{1,0:T(8,128)(2,1)S(1)} %get-tuple-element.30), channel_id=1, source_target_pairs={{0,2},{1,3},{2,0},{3,1},{4,6},{5,7},{6,4},{7,5},{8,10},{9,11},{10,... | collective-permute-start | bytes 835592 | tf_op jit(solution)/shard_map/ppermute | solution.py:42
  26.7 5.5 %collective-permute-start.8 = (bf16[16,2176]{1,0:T(8,128)(2,1)S(1)}, bf16[16,2176]{1,0:T(8,128)(2,1)S(1)}, u32[]{:S(2)}, u32[]{:S(2)}) collective-permute-start(bf16[16,2176]{1,0:T(8,128)(2,1)S(1)} %get-tuple-element.36), channel_id=1, source_target_pairs={{0,5},{1,4},{2,7},{3,6},{4,1},{5,0},{6,3},{7,2},{8,13},{9,12},{10,... | collective-permute-start | bytes 208904 | tf_op jit(solution)/shard_map/ppermute | solution.py:42
  28.2 5.4 %collective-permute-start.9 = (bf16[16,2176]{1,0:T(8,128)(2,1)S(1)}, bf16[16,2176]{1,0:T(8,128)(2,1)S(1)}, u32[]{:S(2)}, u32[]{:S(2)}) collective-permute-start(bf16[16,2176]{1,0:T(8,128)(2,1)S(1)} %get-tuple-element.37), channel_id=1, source_target_pairs={{0,4},{1,5},{2,6},{3,7},{4,0},{5,1},{6,2},{7,3},{8,12},{9,13},{10,... | collective-permute-start | bytes 208904 | tf_op jit(solution)/shard_map/ppermute | solution.py:42
  29.5 4.3 %collective-permute-start.10 = (bf16[16,2176]{1,0:T(8,128)(2,1)S(1)}, bf16[16,2176]{1,0:T(8,128)(2,1)S(1)}, u32[]{:S(2)}, u32[]{:S(2)}) collective-permute-start(bf16[16,2176]{1,0:T(8,128)(2,1)S(1)} %get-tuple-element.38), channel_id=1, source_target_pairs={{0,1},{1,0},{2,3},{3,2},{4,5},{5,4},{6,7},{7,6},{8,9},{9,8},{10,11... | collective-permute-start | bytes 208904 | tf_op jit(solution)/shard_map/ppermute | solution.py:42
  33.9 5.6 %collective-permute-start.11 = (bf16[4,2560]{1,0:T(4,128)(2,1)S(1)}, bf16[4,2560]{1,0:T(4,128)(2,1)S(1)}, u32[]{:S(2)}, u32[]{:S(2)}) collective-permute-start(bf16[4,2560]{1,0:T(4,128)(2,1)S(1)} %get-tuple-element.41), channel_id=1, source_target_pairs={{0,24},{1,25},{2,26},{3,27},{4,28},{5,29},{6,30},{7,31},{8,16},{9,... | collective-permute-start | bytes 61448 | tf_op jit(solution)/shard_map/ppermute | solution.py:42
  35.8 4.7 %collective-permute-start.12 = (bf16[4,2560]{1,0:T(4,128)(2,1)S(1)}, bf16[4,2560]{1,0:T(4,128)(2,1)S(1)}, u32[]{:S(2)}, u32[]{:S(2)}) collective-permute-start(bf16[4,2560]{1,0:T(4,128)(2,1)S(1)} %get-tuple-element.42), channel_id=1, source_target_pairs={{0,16},{1,17},{2,18},{3,19},{4,20},{5,21},{6,22},{7,23},{8,24},{9,... | collective-permute-start | bytes 61448 | tf_op jit(solution)/shard_map/ppermute | solution.py:42
  36.0 4.4 %copy-start = (bf16[2048,16]{0,1:T(8,128)(2,1)S(1)}, bf16[2048,16]{0,1:T(8,128)(2,1)}, u32[]{:S(2)}) copy-start(bf16[2048,16]{0,1:T(8,128)(2,1)} %param.12) | copy-start | bytes 196612
  36.1 4.4 %collective-permute-start.13 = (bf16[4,2560]{1,0:T(4,128)(2,1)S(1)}, bf16[4,2560]{1,0:T(4,128)(2,1)S(1)}, u32[]{:S(2)}, u32[]{:S(2)}) collective-permute-start(bf16[4,2560]{1,0:T(4,128)(2,1)S(1)} %get-tuple-element.43), channel_id=1, source_target_pairs={{0,8},{1,9},{2,10},{3,11},{4,12},{5,13},{6,14},{7,15},{8,0},{9,1},... | collective-permute-start | bytes 61448 | tf_op jit(solution)/shard_map/ppermute | solution.py:42
